TPU v7x, 512 devices: a whole 4x8x8 slice. The times are simulated.
512 devices in a mesh: dp: 8 (over x, z_lo), tensor: 64 (over y, z_hi, core).
Axes of the slice: x: 4, y: 8, z: 8 (z_hi: 4, z_lo: 2; z = z_hi * 2 + z_lo), core: 2. Of those that a mesh axis runs over, the one named last changes fastest.
Arguments:
- tokens_b: bfloat16 [512, 8192], P(('dp', 'tensor')), parts along dimension 0, may hold values from -6 to 6
- tokens_a: bfloat16 [512, 8192], P(('dp', 'tensor')), parts along dimension 0, may hold values from -6 to 6
- grad_out_a: bfloat16 [512, 8192], P(('dp', 'tensor')), parts along dimension 0, may hold values from -6 to 6
- gate_weight: bfloat16 [8192, 26624], P(None, 'tensor'), may hold values from -0.0625 to 0.0625
- up_weight: bfloat16 [8192, 26624], P(None, 'tensor'), may hold values from -0.0625 to 0.0625
- down_weight: bfloat16 [26624, 8192], P('tensor'), may hold values from -0.0390625 to 0.0390625
Outputs:
- output_b: bfloat16 [512, 8192], P(('dp', 'tensor')), parts along dimension 0
- grad_in_a: bfloat16 [512, 8192], P(('dp', 'tensor')), parts along dimension 0
There are 8 independent parts, one for each index of `dp`. A program takes and returns all parts, laid end to end along the dimension named above; an argument that names none is the same for every part. Nothing has to cross between parts.
All inputs are finite; a program needn't handle non-finite values.
Results may differ from a plain program's by a relative error of at most 0.0049.
Values may be sent and summed in bfloat16 or wider, within the bound.
A program may use at most 128 MiB of HBM per device.

v0:
```python
import jax
import jax.numpy as jnp
from jax import lax
from jax.sharding import PartitionSpec as P

contract = (((1,), (1,)), ((), ()))


def local(tokens_b, tokens_a, grad_out_a, gate_weight, up_weight, down_weight):
    piece = lax.all_gather(tokens_b, "tensor", axis=0, tiled=True)
    gate = jnp.dot(piece, gate_weight, preferred_element_type=jnp.float32)
    upper = jnp.dot(piece, up_weight, preferred_element_type=jnp.float32)
    hidden_b = (jax.nn.silu(gate) * upper).astype(jnp.bfloat16)
    all_a, all_grad = (
        lax.all_gather(tokens_a, "tensor", axis=0, tiled=True),
        lax.all_gather(grad_out_a, "tensor", axis=0, tiled=True),
    )
    gate_a = jnp.dot(all_a, gate_weight, preferred_element_type=jnp.float32)
    up_a = jnp.dot(all_a, up_weight, preferred_element_type=jnp.float32)
    grad_hidden = lax.dot_general(
        all_grad, down_weight, contract, preferred_element_type=jnp.float32
    )
    sigma = jax.nn.sigmoid(gate_a)
    grad_gate = (grad_hidden * up_a * sigma * (1.0 + gate_a * (1.0 - sigma))).astype(jnp.bfloat16)
    grad_up = (grad_hidden * gate_a * sigma).astype(jnp.bfloat16)
    output_b = lax.psum_scatter(
        jnp.dot(hidden_b, down_weight, preferred_element_type=jnp.float32),
        "tensor",
        scatter_dimension=0,
        tiled=True,
    )
    total = lax.dot_general(grad_gate, gate_weight, contract, preferred_element_type=jnp.float32)
    grad_in = lax.psum_scatter(
        total + lax.dot_general(grad_up, up_weight, contract, preferred_element_type=jnp.float32),
        "tensor",
        scatter_dimension=0,
        tiled=True,
    )
    return (output_b.astype(jnp.bfloat16), grad_in.astype(jnp.bfloat16))


def solution(mesh):
    return jax.shard_map(
        local,
        mesh=mesh,
        in_specs=(
            P(("dp", "tensor"), None),
            P(("dp", "tensor"), None),
            P(("dp", "tensor"), None),
            P(None, "tensor"),
            P(None, "tensor"),
            P("tensor", None),
        ),
        out_specs=(P(("dp", "tensor"), None), P(("dp", "tensor"), None)),
        check_vma=False,
    )
```

profile of v0, /device:TPU:1, one launch (start us, length us, event | category | flops | bytes accessed | tf_op | source)
XLA Modules:
  0.0 628.3 jit_solution(11949221493604727593)
XLA Ops:
  7.2 0.0 all-gather.11.cloned.1.call-start
  7.2 0.7 all-gather.11.cloned.1.call-update
  7.9 0.0 all-gather.9.cloned.1.call-start
  7.9 0.7 all-gather.9.cloned.1.call-update
  8.6 0.0 all-gather.7.cloned.1.call-start
  8.7 0.7 all-gather.7.cloned.1.call-update
  9.4 1.3 dynamic-slice
  10.7 91.5 %all-gather.11.cloned.1.call-done = bf16[64,1,8192]{2,1,0:T(2,128)(2,1)} async-done(((bf16[1,1,8192]{2,1,0:T(2,128)(2,1)}), bf16[64,1,8192]{2,1,0:T(2,128)(2,1)}) %all-gather.11.cloned.1.call-update) | async-done | bytes 1048592 | tf_op jit(solution)/shard_map/all_gather | solution.py:15
  102.1 0.0 copy-start
  102.1 5.9 fusion.6
  108.1 79.1 %all-gather.9.cloned.1.call-done = bf16[64,1,8192]{2,1,0:T(2,128)(2,1)} async-done(((bf16[1,1,8192]{2,1,0:T(2,128)(2,1)}), bf16[64,1,8192]{2,1,0:T(2,128)(2,1)}) %all-gather.9.cloned.1.call-update) | async-done | bytes 1048592 | tf_op jit(solution)/shard_map/all_gather | solution.py:16
  187.1 5.8 fusion.10
  192.9 0.0 copy-done
  192.9 10.4 %fusion.4 = f32[64,8192]{1,0:T(8,128)} fusion(bf16[8192,416]{0,1:T(8,128)(2,1)} %param.9, f32[64,416]{1,0:T(8,128)S(1)} %fusion.10, bf16[8192,416]{0,1:T(8,128)(2,1)} %param.10, bf16[64,1,8192]{2,1,0:T(2,128)(2,1)S(1)} %copy-done, f32[64,416]{1,0:T(8,128)S(1)} %fusion.6), kind=kOutput, calls=%fused_computation.7 | convolution fusion | flops 872681472 | bytes 16990208 | tf_op jit(solution)/shard_map/dot_general | solution.py:32
  203.3 4.9 convolution_add_fusion
  208.2 63.9 %all-gather.7.cloned.1.call-done = bf16[64,1,8192]{2,1,0:T(2,128)(2,1)} async-done(((bf16[1,1,8192]{2,1,0:T(2,128)(2,1)}), bf16[64,1,8192]{2,1,0:T(2,128)(2,1)}) %all-gather.7.cloned.1.call-update) | async-done | bytes 1048592 | tf_op jit(solution)/shard_map/all_gather | solution.py:10
  272.1 5.8 fusion.15
  277.9 11.1 %fusion.5 = f32[64,8192]{1,0:T(8,128)} fusion(bf16[416,8192]{1,0:T(8,128)(2,1)} %param.11, bf16[8192,416]{0,1:T(8,128)(2,1)} %param.10, bf16[64,1,8192]{2,1,0:T(2,128)(2,1)} %all-gather.7.cloned.1.call-done, f32[64,416]{1,0:T(8,128)S(1)} %fusion.15), kind=kOutput, calls=%fused_computation.8 | convolution fusion | flops 872574976 | bytes 16883712 | tf_op jit(solution)/shard_map/dot_general | solution.py:27
  289.1 330.5 %all-reduce.4 = (bf16[64,8192]{1,0:T(8,128)(2,1)S(1)}, bf16[64,8192]{1,0:T(8,128)(2,1)}) all-reduce(f32[64,8192]{1,0:T(8,128)} %fusion.5, f32[64,8192]{1,0:T(8,128)S(1)} %convolution_add_fusion), channel_id=2, replica_groups=mesh['dp'=8,'tensor'=64] {'tensor'}, use_global_device_ids=true, to_apply=%region_0.1.clone | all-reduce | flops 1048576 | bytes 6291456
  619.6 2.2 dynamic-slice_convert_fusion
Async XLA Ops:
  7.2 95.0 %all-gather.11.cloned.1.call-start = ((), (), s32[]{:S(2)}) async-start(), calls=%async_computation.2 | async-start | bytes 2129920 | tf_op jit(solution)/shard_map/all_gather | solution.py:15
  7.9 179.2 %all-gather.9.cloned.1.call-start = ((), (), s32[]{:S(2)}) async-start(), calls=%async_computation.1 | async-start | bytes 2129920 | tf_op jit(solution)/shard_map/all_gather | solution.py:16
  8.6 263.5 %all-gather.7.cloned.1.call-start = ((), (), s32[]{:S(2)}) async-start(), calls=%async_computation | async-start | bytes 2129920 | tf_op jit(solution)/shard_map/all_gather | solution.py:10
  102.1 90.8 %copy-start = (bf16[64,1,8192]{2,1,0:T(2,128)(2,1)S(1)}, bf16[64,1,8192]{2,1,0:T(2,128)(2,1)}, u32[]{:S(2)}) copy-start(bf16[64,1,8192]{2,1,0:T(2,128)(2,1)} %all-gather.11.cloned.1.call-done) | copy-start | bytes 3145732
Sparse Core Ops, SparseCore 0:
  11.3 90.7 all-gather.10
  105.4 81.6 all-gather.8
  190.5 81.6 all-gather.6
where the time goes:
time: 637 us; the launch traced here: 628 us
  blocking collectives  331 us (52%)
  waiting for transfers between devices  237 us (37%)
  matrix products  43.9 us (7%)
  between operations  13.8 us (2%)
    unnamed x1, blocking collectives  331 us
    all_gather x1, waiting for transfers between devices, local(): lax.all_gather(tokens_a, 'tensor', axis=0, tiled=True)  91.5 us
    all_gather x1, waiting for transfers between devices, local(): lax.all_gather(grad_out_a, 'tensor', axis=0, tiled=True)  79.1 us
    all_gather x1, waiting for transfers between devices, local(): piece = lax.all_gather(tokens_b, 'tensor', axis=0, tiled=True)  63.9 us
  transfers between devices with their start and end apart: 3, of which 3 were waited for; matrix products, arithmetic and copies ran while one was open for 4% of the time, Pallas kernels for 0%

commit v1 on v0

v1 whole, which is shorter than its diff:
```python
import functools

import jax
import jax.numpy as jnp
from jax import lax
from jax.experimental import pallas as pl
from jax.experimental.pallas import tpu as pltpu
from jax.sharding import PartitionSpec as P

MESH = pl.DeviceIdType.MESH
f32, bf16 = jnp.float32, jnp.bfloat16
NT = (((1,), (1,)), ((), ()))
LANES = 128
NY, NZ, NC = 8, 4, 2


def kernel(
    ny, nz, xb, xa, xg, wg_hbm, wu_hbm, wd_hbm, out_b, out_a,
    wg, wu, wd, comm, commg, stage, op_t, op_g, part, psend, precv,
    s1, r1, t1, q1s, q1r, s2, r2, t2, q2s, q2r,
    w_sem, z_s, z_r, ring_s, ring_r, sib_s, sib_r,
    gy_s, gy_r, gz_s, gz_r, gsib_s, gsib_r,
    p_s, p_r, a_s, a_r, b_s, b_r,
):
    d = wg.shape[1]
    rows = d // LANES
    half = rows // 2
    per_core = ny * nz
    tokens = per_core * NC

    t = lax.axis_index("tensor")
    c = lax.rem(t, NC)
    z = lax.rem(lax.div(t, NC), nz)
    y = lax.div(t, NC * nz)

    def at(yy, zz, cc):
        return {"tensor": (yy * nz + zz) * NC + cc}

    def yr(k):
        return lax.rem(y + k, ny)

    def zr(k):
        return lax.rem(z + k, nz)

    sib = at(y, z, 1 - c)
    sent = []

    def send(src, dst, ss, rs, dev):
        cp = pltpu.make_async_remote_copy(
            src_ref=src, dst_ref=dst, send_sem=ss, recv_sem=rs, device_id=dev, device_id_type=MESH
        )
        cp.start()
        sent.append(cp)
        return cp

    loads = [
        pltpu.make_async_copy(h, v, w_sem.at[i])
        for i, (h, v) in enumerate(((wd_hbm, wd), (wg_hbm, wg), (wu_hbm, wu)))
    ]
    for cp in loads:
        cp.start()

    barrier = pltpu.get_barrier_semaphore()
    peers = [at(yr(k), z, c) for k in range(1, ny)] + [at(y, zr(k), c) for k in range(1, nz)] + [sib]
    for dev in peers:
        pl.semaphore_signal(barrier, inc=1, device_id=dev, device_id_type=MESH)

    def own_row(x, dst):
        for s in range(rows):
            stage[s : s + 1, :] = x[0:1, s * LANES : (s + 1) * LANES].astype(f32)
        dst[...] = stage[0:rows, :].astype(bf16)

    zrow = pl.ds(pl.multiple_of(z * rows, rows), rows)
    yrow = pl.ds(pl.multiple_of(y * rows, rows), rows)
    own_row(xg, commg.at[c, z, yrow])
    own_row(xb, comm.at[0, c, y, zrow])
    own_row(xa, comm.at[1, c, y, zrow])
    pl.semaphore_wait(barrier, len(peers))

    gy = []
    zs = [[], []]
    for k in range(1, max(ny, nz)):
        if k < nz:
            for i in range(2):
                ref = comm.at[i, c, y, zrow]
                zs[i].append(send(ref, ref, z_s.at[i, k - 1], z_r.at[i, k - 1], at(y, zr(k), c)))
        if k < ny:
            ref = commg.at[c, z, yrow]
            gy.append(send(ref, ref, gy_s.at[k - 1], gy_r.at[k - 1], at(yr(k), z, c)))

    sibs = [[], []]
    ring = [[[], []], [[], []]]

    def to_sibling(i, k):
        ref = comm.at[i, c, yr(k)]
        sibs[i].append(send(ref, ref, sib_s.at[i, k], sib_r.at[i, k], sib))

    def ring_step(i, way, step):
        k = lax.rem(y + (ny - step if way == 0 else step), ny)
        ref = comm.at[i, c, k]
        dev = at(yr(1 if way == 0 else ny - 1), z, c)
        ring[i][way].append(send(ref, ref, ring_s.at[i, way, step], ring_r.at[i, way, step], dev))

    def steps_of(i, way):
        return ny // 2 - (1 if (i == way) else 0)

    for i in range(2):
        for cp in zs[i]:
            cp.wait_recv()
        for way in range(2):
            ring_step(i, way, 0)
        to_sibling(i, 0)
    for cp in gy:
        cp.wait_recv()
    gz = []
    gsibs = []
    ref = commg.at[c, z]
    for k in range(1, nz):
        gz.append(send(ref, ref, gz_s.at[k - 1], gz_r.at[k - 1], at(y, zr(k), c)))
    gsibs.append(send(ref, ref, gsib_s.at[0], gsib_r.at[0], sib))

    for step in range(ny // 2):
        for i in range(2):
            for way in range(2):
                if step < steps_of(i, way):
                    ring[i][way][step].wait_recv()
                    if step + 1 < steps_of(i, way):
                        ring_step(i, way, step + 1)
                    to_sibling(i, (ny - step - 1) if way == 0 else step + 1)

    for k in range(1, nz):
        gz[k - 1].wait_recv()
        ref = commg.at[c, zr(nz - k)]
        gsibs.append(send(ref, ref, gsib_s.at[k], gsib_r.at[k], sib))

    def to_operand(dst, lo):
        for s in range(rows):
            dst[lo : lo + tokens, s * LANES : (s + 1) * LANES] = stage[
                pl.ds(s, tokens, stride=rows), :
            ].astype(bf16)

    def product(w, v):
        return lax.dot_general(w[...], v, NT, preferred_element_type=f32)

    for i in range(2):
        for cp in sibs[i]:
            cp.wait_recv()
        for cc in range(NC):
            for yy in range(ny):
                lo = (cc * ny + yy) * nz * rows
                stage[lo : lo + nz * rows, :] = comm[i, cc, yy].astype(f32)
        to_operand(op_t, i * tokens)
    loads[1].wait()
    gate = product(wg, op_t[...]).T
    loads[2].wait()
    upper = product(wu, op_t[...]).T
    sigma = jax.nn.sigmoid(gate)
    hidden_b = (gate[:tokens] * sigma[:tokens] * upper[:tokens]).astype(bf16)

    for cp in gsibs:
        cp.wait_recv()
    for cc in range(NC):
        for zz in range(nz):
            for yy in range(ny):
                lo = ((cc * ny + yy) * nz + zz) * rows
                stage[lo : lo + rows, :] = commg[cc, zz, yy * rows : (yy + 1) * rows].astype(f32)
    to_operand(op_g, 0)
    loads[0].wait()
    grad_hidden = product(wd, op_g[...]).T
    gate_a, up_a, sg = gate[tokens:], upper[tokens:], sigma[tokens:]
    grad_gate = (grad_hidden * up_a * sg * (1.0 + gate_a * (1.0 - sg))).astype(bf16)
    grad_up = (grad_hidden * gate_a * sg).astype(bf16)

    width = min(d // 2, 2048)

    def columns(i, h):
        for lo in range(h * (d // 2), (h + 1) * (d // 2), width):
            cut = slice(lo, lo + width)
            if i == 0:
                v = jnp.dot(hidden_b, wd[:, cut], preferred_element_type=f32)
            else:
                v = jnp.dot(grad_gate, wg[:, cut], preferred_element_type=f32)
                v = v + jnp.dot(grad_up, wu[:, cut], preferred_element_type=f32)
            for s in range(width // LANES):
                row = (lo - h * (d // 2)) // LANES + s
                part[i, h, pl.ds(row, tokens, stride=half), :] = v[:, s * LANES : (s + 1) * LANES]

    core_rows = per_core * half

    def pair(i, h):
        lo = pl.multiple_of((1 - c) * core_rows, core_rows)
        psend[i, h] = part[i, h, pl.ds(lo, core_rows), :].astype(bf16)
        return send(psend.at[i, h], precv.at[i, h], p_s.at[i, h], p_r.at[i, h], sib)

    def mine(i, h, lo, n):
        lo = pl.multiple_of(lo, n)
        own = part[i, h, pl.ds(pl.multiple_of(c * core_rows + lo, n), n), :]
        return own + precv[i, h, pl.ds(lo, n), :].astype(f32)

    yb, zb = nz * half, ny * half

    def round_one(i, h, cp):
        cp.wait_recv()
        out = []
        if h == 0:
            for k in range(1, ny):
                s1[i, k - 1] = mine(i, h, yr(k) * yb, yb).astype(bf16)
                out.append(send(s1.at[i, k - 1], r1.at[i, k - 1], a_s.at[i, h, k - 1], a_r.at[i, h, k - 1], at(yr(k), z, c)))
            t1[i] = mine(i, h, y * yb, yb)
        else:
            for k in range(nz):
                for yy in range(ny):
                    v = mine(i, h, (yy * nz + zr(k)) * half, half)
                    if k:
                        s2[i, k - 1, yy * half : (yy + 1) * half, :] = v.astype(bf16)
                    else:
                        t2[i, yy * half : (yy + 1) * half, :] = v
                if k:
                    out.append(send(s2.at[i, k - 1], r2.at[i, k - 1], a_s.at[i, h, k - 1], a_r.at[i, h, k - 1], at(y, zr(k), c)))
        return out

    def round_two(i, h, cps):
        for cp in cps:
            cp.wait_recv()
        out = []
        if h == 0:
            v = t1[i]
            for k in range(ny - 1):
                v = v + r1[i, k].astype(f32)
            t1[i] = v
            for k in range(1, nz):
                q1s[i, k - 1] = t1[i, pl.ds(pl.multiple_of(zr(k) * half, half), half), :].astype(bf16)
                out.append(send(q1s.at[i, k - 1], q1r.at[i, k - 1], b_s.at[i, h, k - 1], b_r.at[i, h, k - 1], at(y, zr(k), c)))
        else:
            v = t2[i]
            for k in range(nz - 1):
                v = v + r2[i, k].astype(f32)
            t2[i] = v
            for k in range(1, ny):
                q2s[i, k - 1] = t2[i, pl.ds(pl.multiple_of(yr(k) * half, half), half), :].astype(bf16)
                out.append(send(q2s.at[i, k - 1], q2r.at[i, k - 1], b_s.at[i, h, k - 1], b_r.at[i, h, k - 1], at(yr(k), z, c)))
        return out

    def finish(i, h, cps):
        for cp in cps:
            cp.wait_recv()
        out = out_b if i == 0 else out_a
        if h == 0:
            v = t1[i, pl.ds(pl.multiple_of(z * half, half), half), :]
            for k in range(nz - 1):
                v = v + q1r[i, k].astype(f32)
        else:
            v = t2[i, pl.ds(pl.multiple_of(y * half, half), half), :]
            for k in range(ny - 1):
                v = v + q2r[i, k].astype(f32)
        out[h * half : (h + 1) * half, :] = v.astype(bf16)

    pairs, ones, twos = {}, {}, {}
    order = [(0, 1), (0, 0), (1, 1), (1, 0)]
    for j, ih in enumerate(order):
        columns(*ih)
        pairs[ih] = pair(*ih)
        if j >= 1:
            ones[order[j - 1]] = round_one(*order[j - 1], pairs[order[j - 1]])
    ones[order[-1]] = round_one(*order[-1], pairs[order[-1]])
    for ih in order:
        twos[ih] = round_two(*ih, ones[ih])
    for ih in order:
        finish(*ih, twos[ih])
    for cp in sent:
        cp.wait_send()


def local(ny, nz, tokens_b, tokens_a, grad_out_a, gate_weight, up_weight, down_weight):
    h, d = down_weight.shape
    rows = d // LANES
    half = rows // 2
    per_core = ny * nz
    tokens = per_core * NC
    vmem, dma = pltpu.VMEM, pltpu.SemaphoreType.DMA
    row = jax.ShapeDtypeStruct((rows, LANES), bf16)
    in_vmem, anywhere = pl.BlockSpec(memory_space=vmem), pl.BlockSpec(memory_space=pl.ANY)
    output_b, grad_in = pl.pallas_call(
        functools.partial(kernel, ny, nz),
        out_shape=(row, row),
        in_specs=[in_vmem] * 3 + [anywhere] * 3,
        out_specs=(in_vmem, in_vmem),
        scratch_shapes=[
            vmem((h, d), bf16),
            vmem((h, d), bf16),
            vmem((h, d), bf16),
            vmem((2, NC, ny, nz * rows, LANES), bf16),
            vmem((NC, nz, ny * rows, LANES), bf16),
            vmem((tokens * rows, LANES), f32),
            vmem((2 * tokens, d), bf16),
            vmem((tokens, d), bf16),
            vmem((2, 2, tokens * half, LANES), f32),
            vmem((2, 2, per_core * half, LANES), bf16),
            vmem((2, 2, per_core * half, LANES), bf16),
            vmem((2, ny - 1, nz * half, LANES), bf16),
            vmem((2, ny - 1, nz * half, LANES), bf16),
            vmem((2, nz * half, LANES), f32),
            vmem((2, nz - 1, half, LANES), bf16),
            vmem((2, nz - 1, half, LANES), bf16),
            vmem((2, nz - 1, ny * half, LANES), bf16),
            vmem((2, nz - 1, ny * half, LANES), bf16),
            vmem((2, ny * half, LANES), f32),
            vmem((2, ny - 1, half, LANES), bf16),
            vmem((2, ny - 1, half, LANES), bf16),
            dma((3,)),
            dma((2, nz - 1)),
            dma((2, nz - 1)),
            dma((2, 2, ny // 2)),
            dma((2, 2, ny // 2)),
            dma((2, ny)),
            dma((2, ny)),
            dma((ny - 1,)),
            dma((ny - 1,)),
            dma((nz - 1,)),
            dma((nz - 1,)),
            dma((nz,)),
            dma((nz,)),
            dma((2, 2)),
            dma((2, 2)),
            dma((2, 2, ny - 1)),
            dma((2, 2, ny - 1)),
            dma((2, 2, ny - 1)),
            dma((2, 2, ny - 1)),
        ],
        compiler_params=pltpu.CompilerParams(
            collective_id=0, has_side_effects=True, vmem_limit_bytes=60 * 2**20
        ),
        cost_estimate=pl.CostEstimate(flops=2 * 8 * tokens * d * h, bytes_accessed=6 * d * h, transcendentals=0),
        name="swiglu",
    )(tokens_b, tokens_a, grad_out_a, gate_weight.T, up_weight.T, down_weight)
    return output_b.reshape(1, d), grad_in.reshape(1, d)


def solution(mesh, ny=NY, nz=NZ):
    row, column = P(("dp", "tensor"), None), P(None, "tensor")
    return jax.shard_map(
        functools.partial(local, ny, nz),
        mesh=mesh,
        in_specs=(row, row, row, column, column, P("tensor", None)),
        out_specs=(row, row),
        check_vma=False,
    )
```

time: 637 us -> 79 us (0.12); the launches traced: 628 us -> 78.4 us
  blocking collectives: 331 us -> 0 us
  waiting for transfers between devices: 237 us -> 0 us
  Pallas kernels: 0 us -> 76.4 us
  matrix products: 43.9 us -> 0 us
  between operations: 13.8 us -> 0.64 us
    unnamed x1 -> x0, blocking collectives: 331 us -> none
    all_gather x3 -> x0, waiting for transfers between devices: 234 us -> none  [the longest x1 91.5 us: local(): lax.all_gather(tokens_a, 'tensor', axis=0, tiled=True)]
    pallas_call x0 -> x1, Pallas kernels: none -> 76.4 us  [local(): pl.pallas_call(functools.partial(kernel, ny, nz), out_shape=(row, row), i...]
    dot_general x6 -> x0, matrix products: 43.9 us -> none  [the longest x1 11.1 us: local(): jnp.dot(hidden_b, down_weight, preferred_element_type=jnp.float32)]
  transfers between devices with their start and end apart: 3 -> 0, of which waited for: 3 -> 0; matrix products, arithmetic and copies ran while one was open for 4% -> 0% of each run, Pallas kernels for 0% -> 0%
where the time goes in v1:
time: 79 us; the launch traced here: 78.4 us
  Pallas kernels  76.4 us (97%)
  local copies, waits for them, and re-layouts  1.41 us (2%)
    pallas_call x1, Pallas kernels, local(): pl.pallas_call(functools.partial(kernel, ny, nz), out_shape=(row, row), i...  76.4 us

profile of v1, /device:TPU:1, one launch (start us, length us, event | category | flops | bytes accessed | tf_op | source)
XLA Modules:
  0.0 78.4 jit_solution(14339896133930076960)
XLA Ops:
  0.6 76.4 %swiglu.1 = (bf16[64,128]{1,0:T(8,128)(2,1)}, bf16[64,128]{1,0:T(8,128)(2,1)}) custom-call(bf16[1,8192]{1,0:T(2,128)(2,1)} %xb.1, bf16[1,8192]{1,0:T(2,128)(2,1)} %xa.1, bf16[1,8192]{1,0:T(2,128)(2,1)} %xg.1, bf16[416,8192]{1,0:T(8,128)(2,1)} %bitcast.10, bf16[416,8192]{1,0:T(8,128)(2,1)} %bitcast.11, bf16[416,8192]{1,0:T(8,128)(2,1)} %wd_hbm.1), custom_call_target="tpu_custom_call" | custom-call | flops 3489660928 | bytes 20447232 | tf_op jit(solution)/shard_map/swiglu/pallas_call | solution.py:283
  77.0 1.4 %copy_bitcast_fusion = (bf16[1,8192]{1,0:T(2,128)(2,1)}, bf16[1,8192]{1,0:T(2,128)(2,1)}) fusion(bf16[1,1,64,128]{3,2,1,0:T(8,128)(2,1)} %bitcast.13, bf16[1,1,64,128]{3,2,1,0:T(8,128)(2,1)} %bitcast.12), kind=kLoop, calls=%fused_computation | loop fusion | bytes 65536 | tf_op jit(solution)/shard_map/reshape | solution.py:336

commit v2 on v0

v2 whole, which is shorter than its diff:
```python
import functools

import jax
import jax.numpy as jnp
from jax import lax
from jax.experimental import pallas as pl
from jax.experimental.pallas import tpu as pltpu
from jax.sharding import PartitionSpec as P

def firsts(n):
    return [2, -2, 1, -1] if n == 8 else [1, -1] if n == 4 else [1]


def seconds(n):
    return [2, -2] if n == 8 else []


def far_first(n):
    return sorted(range(1, n), key=lambda k: -min(k, n - k))


MESH = pl.DeviceIdType.MESH
f32, bf16 = jnp.float32, jnp.bfloat16
NT = (((1,), (1,)), ((), ()))
LANES = 128
PARTS = 4
NY, NZ, NC = 8, 4, 2


def kernel(
    ny, nz, xb, xa, xg, wg_hbm, wu_hbm, wd_hbm, out_b, out_a,
    wg, wu, wd, comm, commg, stage, op_t, op_g, part, psend, precv,
    s1, r1, t1, q1s, q1r, s2, r2, t2, q2s, q2r, w_sem, s_sem, r_sem,
):
    d = wg.shape[1]
    rows = d // LANES
    fine = rows // PARTS
    per_core = ny * nz
    tokens = per_core * NC

    t = lax.axis_index("tensor")
    c = lax.rem(t, NC)
    z = lax.rem(lax.div(t, NC), nz)
    y = lax.div(t, NC * nz)

    def at(yy, zz, cc):
        return {"tensor": (yy * nz + zz) * NC + cc}

    def yr(k):
        return lax.rem(y + k + ny, ny)

    def zr(k):
        return lax.rem(z + k + nz, nz)

    sib = at(y, z, 1 - c)
    sent = []

    def send(src, dst, dev):
        n = len(sent)
        cp = pltpu.make_async_remote_copy(
            src_ref=src, dst_ref=dst, send_sem=s_sem.at[n], recv_sem=r_sem.at[n], device_id=dev, device_id_type=MESH
        )
        cp.start()
        sent.append(cp)
        return cp

    loads = [
        pltpu.make_async_copy(h, v, w_sem.at[i])
        for i, (h, v) in enumerate(((wd_hbm, wd), (wg_hbm, wg), (wu_hbm, wu)))
    ]
    for cp in loads:
        cp.start()

    barrier = pltpu.get_barrier_semaphore()
    peers = [at(yr(k), z, c) for k in range(1, ny)] + [at(y, zr(k), c) for k in range(1, nz)] + [sib]
    for dev in peers:
        pl.semaphore_signal(barrier, inc=1, device_id=dev, device_id_type=MESH)

    def own_row(x, dst):
        for s in range(rows):
            stage[s : s + 1, :] = x[0:1, s * LANES : (s + 1) * LANES].astype(f32)
        dst[...] = stage[0:rows, :].astype(bf16)

    def place(k, n):
        return pl.ds(pl.multiple_of(k * n, n), n)

    own_row(xb, comm.at[c, y, place(2 * z, rows)])
    own_row(xa, comm.at[c, y, place(2 * z + 1, rows)])
    own_row(xg, commg.at[c, z, place(y, rows)])
    pl.semaphore_wait(barrier, len(peers))

    far_y, far_z = far_first(ny), far_first(nz)

    class Tokens:
        def __init__(self):
            self.along_z, self.near, self.far, self.shared = {}, {}, {}, []

        def unit(self, ky, dz):
            return c, ky, place(zr(dz), 2 * rows)

        def go(self, ref, dev):
            return send(ref, ref, dev)

        def share(self, ky, dz):
            self.shared.append(self.go(comm.at[self.unit(ky, dz)], sib))

        def start(self):
            for k in far_z:
                self.along_z[k] = self.go(comm.at[self.unit(y, 0)], at(y, zr(k), c))

        def first(self, dz):
            if dz:
                self.along_z[(nz - dz) % nz].wait_recv()
            for k in firsts(ny):
                self.near[dz, k] = self.go(comm.at[self.unit(y, dz)], at(yr(k), z, c))
            self.share(y, dz)

        def second(self, dz):
            for k in seconds(ny):
                self.near[dz, k].wait_recv()
                one = place(2 * zr(dz) + (0 if k > 0 else 1), rows)
                self.far[dz, 2 * k] = self.go(comm.at[c, yr(-k), one], at(yr(k), z, c))
                self.far[dz, 3 * k // 2] = self.go(comm.at[self.unit(yr(-k), dz)], at(yr(k // 2), z, c))
                self.share(yr(-k), dz)

        def finish(self, dz):
            for k in firsts(ny):
                if k not in seconds(ny):
                    self.near[dz, k].wait_recv()
                    self.share(yr(-k), dz)
            for k in seconds(ny):
                self.far[dz, 3 * k // 2].wait_recv()
                self.share(yr(-3 * k // 2), dz)
            if seconds(ny):
                self.far[dz, 4].wait_recv()
                self.far[dz, -4].wait_recv()
                self.share(yr(4), dz)

        def to_operand(self):
            for cp in self.shared:
                cp.wait_recv()
            for cc in range(NC):
                for yy in range(ny):
                    for j in range(2 * nz):
                        lo = ((j % 2 * NC + cc) * ny + yy) * nz * rows + j // 2 * rows
                        stage[lo : lo + rows, :] = comm[cc, yy, j * rows : (j + 1) * rows].astype(f32)
            to_operand(op_t, 2 * tokens)

    class Cotangents:
        def __init__(self):
            self.along_y, self.up, self.down, self.shared = [], [], [], []

        def piece(self, k, p):
            n = ny * rows // 2
            return commg.at[c, k, pl.ds(p * n, n)]

        def go(self, k, p, dz):
            ref = self.piece(k, p)
            return send(ref, ref, at(y, zr(dz), c))

        def share(self, k, p):
            ref = self.piece(k, p)
            self.shared.append(send(ref, ref, sib))

        def start(self):
            for k in far_y:
                ref = commg.at[c, z, place(y, rows)]
                self.along_y.append(send(ref, ref, at(yr(k), z, c)))

        def first(self):
            for cp in self.along_y:
                cp.wait_recv()
            for p in range(2):
                self.up.append(self.go(z, p, 1))
                self.down.append(self.go(z, 1 - p, -1))
            for p in range(2):
                self.share(z, p)

        def second(self):
            self.up[0].wait_recv()
            self.up.append(self.go(zr(-1), 0, 1))
            self.share(zr(-1), 0)
            self.down[0].wait_recv()
            self.down.append(self.go(zr(1), 1, -1))
            self.share(zr(1), 1)

        def finish(self):
            self.up[1].wait_recv()
            self.share(zr(-1), 1)
            self.down[1].wait_recv()
            self.share(zr(1), 0)
            self.up[2].wait_recv()
            self.share(zr(2), 0)
            self.down[2].wait_recv()
            self.share(zr(2), 1)

        def to_operand(self):
            for cp in self.shared:
                cp.wait_recv()
            for cc in range(NC):
                for zz in range(nz):
                    for yy in range(ny):
                        lo = ((cc * ny + yy) * nz + zz) * rows
                        stage[lo : lo + rows, :] = commg[cc, zz, yy * rows : (yy + 1) * rows].astype(f32)
            to_operand(op_g, tokens)

    def to_operand(op, n):
        for s in range(rows):
            op[:, s * LANES : (s + 1) * LANES] = stage[pl.ds(s, n, stride=rows), :].astype(bf16)

    def product(w, op):
        return lax.dot_general(op[...], w[...], NT, preferred_element_type=f32)

    width = d // PARTS
    both = 2 * fine
    core_rows = per_core * both
    yb = nz * both

    class Part:
        def __init__(self, q, left_b, left_a):
            self.q, self.b, self.z_first = q, q // 2, q % 2 == 0
            for i, pairs_of in enumerate((left_b, left_a)):
                v = sum(
                    jnp.dot(left, w[:, q * width : (q + 1) * width], preferred_element_type=f32)
                    for left, w in pairs_of
                )
                for s in range(fine):
                    part[q, pl.ds(i * fine + s, tokens, stride=both), :] = v[:, s * LANES : (s + 1) * LANES]
            psend[q] = part[q, place(1 - c, core_rows), :].astype(bf16)
            self.pair = send(psend.at[q], precv.at[q], sib)

        def mine(self, lo, n):
            lo = pl.multiple_of(lo, n)
            own = part[self.q, pl.ds(pl.multiple_of(c * core_rows + lo, n), n)]
            return own + precv[self.q, pl.ds(lo, n)].astype(f32)

        def one(self):
            self.pair.wait_recv()
            self.cps = []
            b = self.b
            if self.z_first:
                for k in far_z + [0]:
                    for yy in range(ny):
                        v = self.mine((yy * nz + zr(k)) * both, both)
                        if k:
                            s2[b, k - 1, yy * both : (yy + 1) * both] = v.astype(bf16)
                        else:
                            t2[b, yy * both : (yy + 1) * both] = v
                    if k:
                        self.cps.append(send(s2.at[b, k - 1], r2.at[b, k - 1], at(y, zr(k), c)))
            else:
                for k in far_y:
                    s1[b, k - 1] = self.mine(yr(k) * yb, yb).astype(bf16)
                    self.cps.append(send(s1.at[b, k - 1], r1.at[b, k - 1], at(yr(k), z, c)))
                t1[b] = self.mine(y * yb, yb)

        def two(self):
            for cp in self.cps:
                cp.wait_recv()
            self.cps = []
            b = self.b
            if self.z_first:
                v = t2[b]
                for k in range(nz - 1):
                    v = v + r2[b, k].astype(f32)
                t2[b] = v
                for k in far_y:
                    q2s[b, k - 1] = t2[b, place(yr(k), both)].astype(bf16)
                    self.cps.append(send(q2s.at[b, k - 1], q2r.at[b, k - 1], at(yr(k), z, c)))
            else:
                v = t1[b]
                for k in range(ny - 1):
                    v = v + r1[b, k].astype(f32)
                t1[b] = v
                for k in far_z:
                    q1s[b, k - 1] = t1[b, place(zr(k), both)].astype(bf16)
                    self.cps.append(send(q1s.at[b, k - 1], q1r.at[b, k - 1], at(y, zr(k), c)))

        def finish(self):
            for cp in self.cps:
                cp.wait_recv()
            b = self.b
            if self.z_first:
                v = t2[b, place(y, both)]
                for k in range(ny - 1):
                    v = v + q2r[b, k].astype(f32)
            else:
                v = t1[b, place(z, both)]
                for k in range(nz - 1):
                    v = v + q1r[b, k].astype(f32)
            lo = self.q * fine
            out_b[lo : lo + fine, :] = v[:fine].astype(bf16)
            out_a[lo : lo + fine, :] = v[fine:].astype(bf16)

    tt, tg = Tokens(), Cotangents()
    tt.start()
    tg.start()
    tt.first(0)
    tt.first(-1)
    tt.first(1)
    tt.second(0)
    tt.first(2)
    tg.first()
    tt.second(-1)
    tt.second(1)
    tg.second()
    tt.second(2)
    for dz in (0, -1, 1):
        tt.finish(dz)
    tg.finish()
    tt.finish(2)

    tg.to_operand()
    loads[0].wait()
    grad_hidden = product(wd, op_g)
    tt.to_operand()
    loads[1].wait()
    gate = product(wg, op_t)
    loads[2].wait()
    upper = product(wu, op_t)
    sigma = jax.nn.sigmoid(gate)
    hidden_b = (gate[:tokens] * sigma[:tokens] * upper[:tokens]).astype(bf16)
    gate, upper, sigma = gate[tokens:], upper[tokens:], sigma[tokens:]
    grad_gate = (grad_hidden * upper * sigma * (1.0 + gate * (1.0 - sigma))).astype(bf16)
    grad_up = (grad_hidden * gate * sigma).astype(bf16)
    left_b, left_a = [(hidden_b, wd)], [(grad_gate, wg), (grad_up, wu)]
    parts = []
    for q in range(PARTS):
        parts.append(Part(q, left_b, left_a))
        if q:
            parts[q - 1].one()
    parts[-1].one()
    for p in parts:
        p.two()
    for p in parts:
        p.finish()
    for cp in sent:
        cp.wait_send()


def local(ny, nz, tokens_b, tokens_a, grad_out_a, gate_weight, up_weight, down_weight):
    h, d = down_weight.shape
    rows = d // LANES
    both = 2 * (rows // PARTS)
    per_core = ny * nz
    tokens = per_core * NC
    vmem, dma = pltpu.VMEM, pltpu.SemaphoreType.DMA
    row = jax.ShapeDtypeStruct((rows, LANES), bf16)
    in_vmem, anywhere = pl.BlockSpec(memory_space=vmem), pl.BlockSpec(memory_space=pl.ANY)
    output_b, grad_in = pl.pallas_call(
        functools.partial(kernel, ny, nz),
        out_shape=(row, row),
        in_specs=[in_vmem] * 3 + [anywhere] * 3,
        out_specs=(in_vmem, in_vmem),
        scratch_shapes=[
            vmem((h, d), bf16),
            vmem((h, d), bf16),
            vmem((h, d), bf16),
            vmem((NC, ny, 2 * nz * rows, LANES), bf16),
            vmem((NC, nz, ny * rows, LANES), bf16),
            vmem((2 * tokens * rows, LANES), f32),
            vmem((2 * tokens, d), bf16),
            vmem((tokens, d), bf16),
            vmem((PARTS, tokens * both, LANES), f32),
            vmem((PARTS, per_core * both, LANES), bf16),
            vmem((PARTS, per_core * both, LANES), bf16),
            vmem((2, ny - 1, nz * both, LANES), bf16),
            vmem((2, ny - 1, nz * both, LANES), bf16),
            vmem((2, nz * both, LANES), f32),
            vmem((2, nz - 1, both, LANES), bf16),
            vmem((2, nz - 1, both, LANES), bf16),
            vmem((2, nz - 1, ny * both, LANES), bf16),
            vmem((2, nz - 1, ny * both, LANES), bf16),
            vmem((2, ny * both, LANES), f32),
            vmem((2, ny - 1, both, LANES), bf16),
            vmem((2, ny - 1, both, LANES), bf16),
            dma((3,)),
            dma((160,)),
            dma((160,)),
        ],
        compiler_params=pltpu.CompilerParams(
            collective_id=0, has_side_effects=True, vmem_limit_bytes=60 * 2**20
        ),
        cost_estimate=pl.CostEstimate(flops=2 * 8 * tokens * d * h, bytes_accessed=6 * d * h, transcendentals=0),
        name="swiglu",
    )(tokens_b, tokens_a, grad_out_a, gate_weight.T, up_weight.T, down_weight)
    return output_b.reshape(1, d), grad_in.reshape(1, d)


def solution(mesh, ny=NY, nz=NZ):
    row, column = P(("dp", "tensor"), None), P(None, "tensor")
    return jax.shard_map(
        functools.partial(local, ny, nz),
        mesh=mesh,
        in_specs=(row, row, row, column, column, P("tensor", None)),
        out_specs=(row, row),
        check_vma=False,
    )
```

time: 637 us -> 75.3 us (0.12); the launches traced: 628 us -> 74.9 us
  blocking collectives: 331 us -> 0 us
  waiting for transfers between devices: 237 us -> 0 us
  Pallas kernels: 0 us -> 72.8 us
  matrix products: 43.9 us -> 0 us
  between operations: 13.8 us -> 0.64 us
    unnamed x1 -> x0, blocking collectives: 331 us -> none
    all_gather x3 -> x0, waiting for transfers between devices: 234 us -> none  [the longest x1 91.5 us: local(): lax.all_gather(tokens_a, 'tensor', axis=0, tiled=True)]
    pallas_call x0 -> x1, Pallas kernels: none -> 72.8 us  [local(): pl.pallas_call(functools.partial(kernel, ny, nz), out_shape=(row, row), i...]
    dot_general x6 -> x0, matrix products: 43.9 us -> none  [the longest x1 11.1 us: local(): jnp.dot(hidden_b, down_weight, preferred_element_type=jnp.float32)]
  transfers between devices with their start and end apart: 3 -> 0, of which waited for: 3 -> 0; matrix products, arithmetic and copies ran while one was open for 4% -> 0% of each run, Pallas kernels for 0% -> 0%
where the time goes in v2:
time: 75.3 us; the launch traced here: 74.9 us
  Pallas kernels  72.8 us (97%)
  local copies, waits for them, and re-layouts  1.41 us (2%)
    pallas_call x1, Pallas kernels, local(): pl.pallas_call(functools.partial(kernel, ny, nz), out_shape=(row, row), i...  72.8 us

profile of v2, /device:TPU:1, one launch (start us, length us, event | category | flops | bytes accessed | tf_op | source)
XLA Modules:
  0.0 74.9 jit_solution(1093499854845569941)
XLA Ops:
  0.6 72.8 %swiglu.1 = (bf16[64,128]{1,0:T(8,128)(2,1)}, bf16[64,128]{1,0:T(8,128)(2,1)}) custom-call(bf16[1,8192]{1,0:T(2,128)(2,1)} %xb.1, bf16[1,8192]{1,0:T(2,128)(2,1)} %xa.1, bf16[1,8192]{1,0:T(2,128)(2,1)} %xg.1, bf16[416,8192]{1,0:T(8,128)(2,1)} %bitcast.10, bf16[416,8192]{1,0:T(8,128)(2,1)} %bitcast.11, bf16[416,8192]{1,0:T(8,128)(2,1)} %wd_hbm.1), custom_call_target="tpu_custom_call" | custom-call | flops 3489660928 | bytes 20447232 | tf_op jit(solution)/shard_map/swiglu/pallas_call | solution.py:350
  73.4 1.4 %copy_bitcast_fusion = (bf16[1,8192]{1,0:T(2,128)(2,1)}, bf16[1,8192]{1,0:T(2,128)(2,1)}) fusion(bf16[1,1,64,128]{3,2,1,0:T(8,128)(2,1)} %bitcast.13, bf16[1,1,64,128]{3,2,1,0:T(8,128)(2,1)} %bitcast.12), kind=kLoop, calls=%fused_computation | loop fusion | bytes 65536 | tf_op jit(solution)/shard_map/reshape | solution.py:387

commit v3 on v2

--- a/solution.py
+++ b/solution.py
@@ -66,7 +66,7 @@
 
     loads = [
         pltpu.make_async_copy(h, v, w_sem.at[i])
-        for i, (h, v) in enumerate(((wd_hbm, wd), (wg_hbm, wg), (wu_hbm, wu)))
+        for i, (h, v) in enumerate(((wg_hbm, wg), (wu_hbm, wu), (wd_hbm, wd)))
     ]
     for cp in loads:
         cp.start()
@@ -212,85 +212,81 @@
         return lax.dot_general(op[...], w[...], NT, preferred_element_type=f32)
 
     width = d // PARTS
-    both = 2 * fine
-    core_rows = per_core * both
-    yb = nz * both
+    core_rows = per_core * fine
+    yb = nz * fine
 
     class Part:
-        def __init__(self, q, left_b, left_a):
-            self.q, self.b, self.z_first = q, q // 2, q % 2 == 0
-            for i, pairs_of in enumerate((left_b, left_a)):
-                v = sum(
-                    jnp.dot(left, w[:, q * width : (q + 1) * width], preferred_element_type=f32)
-                    for left, w in pairs_of
-                )
-                for s in range(fine):
-                    part[q, pl.ds(i * fine + s, tokens, stride=both), :] = v[:, s * LANES : (s + 1) * LANES]
-            psend[q] = part[q, place(1 - c, core_rows), :].astype(bf16)
-            self.pair = send(psend.at[q], precv.at[q], sib)
+        def __init__(self, i, q, pairs_of):
+            self.at, self.buf, self.z_first = (i, q), (i, q // 2), q % 2 == 0
+            v = sum(
+                jnp.dot(left, w[:, q * width : (q + 1) * width], preferred_element_type=f32) for left, w in pairs_of
+            )
+            for s in range(fine):
+                part[i, q, pl.ds(s, tokens, stride=fine), :] = v[:, s * LANES : (s + 1) * LANES]
+            psend[i, q] = part[i, q, place(1 - c, core_rows), :].astype(bf16)
+            self.pair = send(psend.at[i, q], precv.at[i, q], sib)
 
         def mine(self, lo, n):
             lo = pl.multiple_of(lo, n)
-            own = part[self.q, pl.ds(pl.multiple_of(c * core_rows + lo, n), n)]
-            return own + precv[self.q, pl.ds(lo, n)].astype(f32)
+            own = part[(*self.at, pl.ds(pl.multiple_of(c * core_rows + lo, n), n))]
+            return own + precv[(*self.at, pl.ds(lo, n))].astype(f32)
 
         def one(self):
             self.pair.wait_recv()
             self.cps = []
-            b = self.b
+            b = self.buf
             if self.z_first:
                 for k in far_z + [0]:
                     for yy in range(ny):
-                        v = self.mine((yy * nz + zr(k)) * both, both)
+                        v = self.mine((yy * nz + zr(k)) * fine, fine)
                         if k:
-                            s2[b, k - 1, yy * both : (yy + 1) * both] = v.astype(bf16)
+                            s2[(*b, k - 1, slice(yy * fine, (yy + 1) * fine))] = v.astype(bf16)
                         else:
-                            t2[b, yy * both : (yy + 1) * both] = v
+                            t2[(*b, slice(yy * fine, (yy + 1) * fine))] = v
                     if k:
-                        self.cps.append(send(s2.at[b, k - 1], r2.at[b, k - 1], at(y, zr(k), c)))
+                        self.cps.append(send(s2.at[(*b, k - 1)], r2.at[(*b, k - 1)], at(y, zr(k), c)))
             else:
                 for k in far_y:
-                    s1[b, k - 1] = self.mine(yr(k) * yb, yb).astype(bf16)
-                    self.cps.append(send(s1.at[b, k - 1], r1.at[b, k - 1], at(yr(k), z, c)))
+                    s1[(*b, k - 1)] = self.mine(yr(k) * yb, yb).astype(bf16)
+                    self.cps.append(send(s1.at[(*b, k - 1)], r1.at[(*b, k - 1)], at(yr(k), z, c)))
                 t1[b] = self.mine(y * yb, yb)
 
         def two(self):
             for cp in self.cps:
                 cp.wait_recv()
             self.cps = []
-            b = self.b
+            b = self.buf
             if self.z_first:
                 v = t2[b]
                 for k in range(nz - 1):
-                    v = v + r2[b, k].astype(f32)
+                    v = v + r2[(*b, k)].astype(f32)
                 t2[b] = v
                 for k in far_y:
-                    q2s[b, k - 1] = t2[b, place(yr(k), both)].astype(bf16)
-                    self.cps.append(send(q2s.at[b, k - 1], q2r.at[b, k - 1], at(yr(k), z, c)))
+                    q2s[(*b, k - 1)] = t2[(*b, place(yr(k), fine))].astype(bf16)
+                    self.cps.append(send(q2s.at[(*b, k - 1)], q2r.at[(*b, k - 1)], at(yr(k), z, c)))
             else:
                 v = t1[b]
                 for k in range(ny - 1):
-                    v = v + r1[b, k].astype(f32)
+                    v = v + r1[(*b, k)].astype(f32)
                 t1[b] = v
                 for k in far_z:
-                    q1s[b, k - 1] = t1[b, place(zr(k), both)].astype(bf16)
-                    self.cps.append(send(q1s.at[b, k - 1], q1r.at[b, k - 1], at(y, zr(k), c)))
+                    q1s[(*b, k - 1)] = t1[(*b, place(zr(k), fine))].astype(bf16)
+                    self.cps.append(send(q1s.at[(*b, k - 1)], q1r.at[(*b, k - 1)], at(y, zr(k), c)))
 
         def finish(self):
             for cp in self.cps:
                 cp.wait_recv()
-            b = self.b
+            b = self.buf
             if self.z_first:
-                v = t2[b, place(y, both)]
+                v = t2[(*b, place(y, fine))]
                 for k in range(ny - 1):
-                    v = v + q2r[b, k].astype(f32)
+                    v = v + q2r[(*b, k)].astype(f32)
             else:
-                v = t1[b, place(z, both)]
+                v = t1[(*b, place(z, fine))]
                 for k in range(nz - 1):
-                    v = v + q1r[b, k].astype(f32)
-            lo = self.q * fine
-            out_b[lo : lo + fine, :] = v[:fine].astype(bf16)
-            out_a[lo : lo + fine, :] = v[fine:].astype(bf16)
+                    v = v + q1r[(*b, k)].astype(f32)
+            i, q = self.at
+            (out_b, out_a)[i][q * fine : (q + 1) * fine, :] = v.astype(bf16)
 
     tt, tg = Tokens(), Cotangents()
     tt.start()
@@ -298,8 +294,8 @@
     tt.first(0)
     tt.first(-1)
     tt.first(1)
+    tt.first(2)
     tt.second(0)
-    tt.first(2)
     tg.first()
     tt.second(-1)
     tt.second(1)
@@ -310,29 +306,34 @@
     tg.finish()
     tt.finish(2)
 
-    tg.to_operand()
+    tt.to_operand()
     loads[0].wait()
-    grad_hidden = product(wd, op_g)
-    tt.to_operand()
+    gate = product(wg, op_t)
     loads[1].wait()
-    gate = product(wg, op_t)
-    loads[2].wait()
     upper = product(wu, op_t)
     sigma = jax.nn.sigmoid(gate)
     hidden_b = (gate[:tokens] * sigma[:tokens] * upper[:tokens]).astype(bf16)
     gate, upper, sigma = gate[tokens:], upper[tokens:], sigma[tokens:]
+    loads[2].wait()
+    parts_b = [Part(0, q, [(hidden_b, wd)]) for q in range(PARTS)]
+    parts_b[0].one()
+    parts_b[1].one()
+    tg.to_operand()
+    parts_b[2].one()
+    parts_b[3].one()
+    grad_hidden = product(wd, op_g)
     grad_gate = (grad_hidden * upper * sigma * (1.0 + gate * (1.0 - sigma))).astype(bf16)
     grad_up = (grad_hidden * gate * sigma).astype(bf16)
-    left_b, left_a = [(hidden_b, wd)], [(grad_gate, wg), (grad_up, wu)]
-    parts = []
+    left_a = [(grad_gate, wg), (grad_up, wu)]
+    parts_a = []
     for q in range(PARTS):
-        parts.append(Part(q, left_b, left_a))
+        parts_a.append(Part(1, q, left_a))
         if q:
-            parts[q - 1].one()
-    parts[-1].one()
-    for p in parts:
+            parts_a[q - 1].one()
+    parts_a[-1].one()
+    for p in parts_b + parts_a:
         p.two()
-    for p in parts:
+    for p in parts_b + parts_a:
         p.finish()
     for cp in sent:
         cp.wait_send()
@@ -341,7 +342,7 @@
 def local(ny, nz, tokens_b, tokens_a, grad_out_a, gate_weight, up_weight, down_weight):
     h, d = down_weight.shape
     rows = d // LANES
-    both = 2 * (rows // PARTS)
+    fine = rows // PARTS
     per_core = ny * nz
     tokens = per_core * NC
     vmem, dma = pltpu.VMEM, pltpu.SemaphoreType.DMA
@@ -361,22 +362,22 @@
             vmem((2 * tokens * rows, LANES), f32),
             vmem((2 * tokens, d), bf16),
             vmem((tokens, d), bf16),
-            vmem((PARTS, tokens * both, LANES), f32),
-            vmem((PARTS, per_core * both, LANES), bf16),
-            vmem((PARTS, per_core * both, LANES), bf16),
-            vmem((2, ny - 1, nz * both, LANES), bf16),
-            vmem((2, ny - 1, nz * both, LANES), bf16),
-            vmem((2, nz * both, LANES), f32),
-            vmem((2, nz - 1, both, LANES), bf16),
-            vmem((2, nz - 1, both, LANES), bf16),
-            vmem((2, nz - 1, ny * both, LANES), bf16),
-            vmem((2, nz - 1, ny * both, LANES), bf16),
-            vmem((2, ny * both, LANES), f32),
-            vmem((2, ny - 1, both, LANES), bf16),
-            vmem((2, ny - 1, both, LANES), bf16),
+            vmem((2, PARTS, tokens * fine, LANES), f32),
+            vmem((2, PARTS, per_core * fine, LANES), bf16),
+            vmem((2, PARTS, per_core * fine, LANES), bf16),
+            vmem((2, 2, ny - 1, nz * fine, LANES), bf16),
+            vmem((2, 2, ny - 1, nz * fine, LANES), bf16),
+            vmem((2, 2, nz * fine, LANES), f32),
+            vmem((2, 2, nz - 1, fine, LANES), bf16),
+            vmem((2, 2, nz - 1, fine, LANES), bf16),
+            vmem((2, 2, nz - 1, ny * fine, LANES), bf16),
+            vmem((2, 2, nz - 1, ny * fine, LANES), bf16),
+            vmem((2, 2, ny * fine, LANES), f32),
+            vmem((2, 2, ny - 1, fine, LANES), bf16),
+            vmem((2, 2, ny - 1, fine, LANES), bf16),
             dma((3,)),
-            dma((160,)),
-            dma((160,)),
+            dma((192,)),
+            dma((192,)),
         ],
         compiler_params=pltpu.CompilerParams(
             collective_id=0, has_side_effects=True, vmem_limit_bytes=60 * 2**20

time: 75.3 us -> 71.6 us (0.951)
  Pallas kernels: 72.8 us -> 69.3 us
    pallas_call x1, Pallas kernels: 72.8 us -> 69.3 us  [local(): pl.pallas_call(functools.partial(kernel, ny, nz), out_shape=(row, row), i...]
where the time goes in v3:
time: 71.6 us; the launch traced here: 71.3 us
  Pallas kernels  69.3 us (97%)
  local copies, waits for them, and re-layouts  1.41 us (2%)
    pallas_call x1, Pallas kernels, local(): pl.pallas_call(functools.partial(kernel, ny, nz), out_shape=(row, row), i...  69.3 us

profile of v3, /device:TPU:1, one launch (start us, length us, event | category | flops | bytes accessed | tf_op | source)
XLA Modules:
  0.0 71.3 jit_solution(5419787005321619626)
XLA Ops:
  0.6 69.3 %swiglu.1 = (bf16[64,128]{1,0:T(8,128)(2,1)}, bf16[64,128]{1,0:T(8,128)(2,1)}) custom-call(bf16[1,8192]{1,0:T(2,128)(2,1)} %xb.1, bf16[1,8192]{1,0:T(2,128)(2,1)} %xa.1, bf16[1,8192]{1,0:T(2,128)(2,1)} %xg.1, bf16[416,8192]{1,0:T(8,128)(2,1)} %bitcast.10, bf16[416,8192]{1,0:T(8,128)(2,1)} %bitcast.11, bf16[416,8192]{1,0:T(8,128)(2,1)} %wd_hbm.1), custom_call_target="tpu_custom_call" | custom-call | flops 3489660928 | bytes 20447232 | tf_op jit(solution)/shard_map/swiglu/pallas_call | solution.py:351
  69.9 1.4 %copy_bitcast_fusion = (bf16[1,8192]{1,0:T(2,128)(2,1)}, bf16[1,8192]{1,0:T(2,128)(2,1)}) fusion(bf16[1,1,64,128]{3,2,1,0:T(8,128)(2,1)} %bitcast.13, bf16[1,1,64,128]{3,2,1,0:T(8,128)(2,1)} %bitcast.12), kind=kLoop, calls=%fused_computation | loop fusion | bytes 65536 | tf_op jit(solution)/shard_map/reshape | solution.py:388

commit v4 on v3

--- a/solution.py
+++ b/solution.py
@@ -93,7 +93,7 @@
 
     class Tokens:
         def __init__(self):
-            self.along_z, self.near, self.far, self.shared = {}, {}, {}, []
+            self.along_z, self.near, self.far, self.shared = {}, {}, {}, {}
 
         def unit(self, ky, dz):
             return c, ky, place(zr(dz), 2 * rows)
@@ -102,7 +102,7 @@
             return send(ref, ref, dev)
 
         def share(self, ky, dz):
-            self.shared.append(self.go(comm.at[self.unit(ky, dz)], sib))
+            self.shared.setdefault(dz, []).append(self.go(comm.at[self.unit(ky, dz)], sib))
 
         def start(self):
             for k in far_z:
@@ -137,13 +137,14 @@
                 self.share(yr(4), dz)
 
         def to_operand(self):
-            for cp in self.shared:
-                cp.wait_recv()
-            for cc in range(NC):
-                for yy in range(ny):
-                    for j in range(2 * nz):
-                        lo = ((j % 2 * NC + cc) * ny + yy) * nz * rows + j // 2 * rows
-                        stage[lo : lo + rows, :] = comm[cc, yy, j * rows : (j + 1) * rows].astype(f32)
+            for dz, cps in self.shared.items():
+                for cp in cps:
+                    cp.wait_recv()
+                for cc in range(NC):
+                    for yy in range(ny):
+                        for j in range(2):
+                            lo = ((j * NC + cc) * ny + yy) * nz + zr(dz)
+                            stage[place(lo, rows), :] = comm[cc, yy, place(2 * zr(dz) + j, rows)].astype(f32)
             to_operand(op_t, 2 * tokens)
 
     class Cotangents:

time: 71.6 us -> 71.4 us (level)
  no operation moved by 1% of the time
where the time goes in v4:
time: 71.4 us; the launch traced here: 71.1 us
  Pallas kernels  69.1 us (97%)
  local copies, waits for them, and re-layouts  1.41 us (2%)
    pallas_call x1, Pallas kernels, local(): pl.pallas_call(functools.partial(kernel, ny, nz), out_shape=(row, row), i...  69.1 us

profile of v4, /device:TPU:1, one launch (start us, length us, event | category | flops | bytes accessed | tf_op | source)
XLA Modules:
  0.0 71.1 jit_solution(10989535147743278891)
XLA Ops:
  0.6 69.1 %swiglu.1 = (bf16[64,128]{1,0:T(8,128)(2,1)}, bf16[64,128]{1,0:T(8,128)(2,1)}) custom-call(bf16[1,8192]{1,0:T(2,128)(2,1)} %xb.1, bf16[1,8192]{1,0:T(2,128)(2,1)} %xa.1, bf16[1,8192]{1,0:T(2,128)(2,1)} %xg.1, bf16[416,8192]{1,0:T(8,128)(2,1)} %bitcast.10, bf16[416,8192]{1,0:T(8,128)(2,1)} %bitcast.11, bf16[416,8192]{1,0:T(8,128)(2,1)} %wd_hbm.1), custom_call_target="tpu_custom_call" | custom-call | flops 3489660928 | bytes 20447232 | tf_op jit(solution)/shard_map/swiglu/pallas_call | solution.py:352
  69.7 1.4 %copy_bitcast_fusion = (bf16[1,8192]{1,0:T(2,128)(2,1)}, bf16[1,8192]{1,0:T(2,128)(2,1)}) fusion(bf16[1,1,64,128]{3,2,1,0:T(8,128)(2,1)} %bitcast.13, bf16[1,1,64,128]{3,2,1,0:T(8,128)(2,1)} %bitcast.12), kind=kLoop, calls=%fused_computation | loop fusion | bytes 65536 | tf_op jit(solution)/shard_map/reshape | solution.py:389
